TPU v7x, 32 devices: a whole 2x2x4 slice. The times are simulated.
32 devices in a mesh: groups: 2 (over y), region: 4 (over z), sub: 2 (over x), lane: 2 (over core).
Axes of the slice: x: 2, y: 2, z: 4, core: 2. Of those that a mesh axis runs over, the one named last changes fastest.
Arguments:
- features: bfloat16 [32, 16, 16, 1024], P(None, 'sub', 'lane', ('groups', 'region')), parts along dimension 3, may hold values from -6 to 6
- occupancy: int32 [16, 16, 1024], P('sub', 'lane', ('groups', 'region')), parts along dimension 2, may hold values 0 or 1
- brick_list: int32 [8, 2, 2, 8], P(('groups', 'region'), 'sub', 'lane'), parts along dimension 0, may hold values from 0 to 15, as said below
- brick_count: int32 [8, 2, 2], P(('groups', 'region'), 'sub', 'lane'), parts along dimension 0, may hold values from 0 to 8, as said below
- weight_one: bfloat16 [27, 32, 32], replicated, may hold values from -0.21875 to 0.21875
- scale_one: float32 [32], replicated, may hold values from 0.25 to 1.75
- shift_one: float32 [32], replicated, may hold values from -3 to 3
- weight_two: bfloat16 [27, 32, 32], replicated, may hold values from -0.21875 to 0.21875
- scale_two: float32 [32], replicated, may hold values from 0.25 to 1.75
- shift_two: float32 [32], replicated, may hold values from -3 to 3
Outputs:
- output: bfloat16 [32, 16, 16, 1024], P(None, 'sub', 'lane', ('groups', 'region')), parts along dimension 3
There are 2 independent parts, one for each index of `groups`. A program takes and returns all parts, laid end to end along the dimension named above; an argument that names none is the same for every part. Nothing has to cross between parts.
Inputs may be any that keep to these rules, and one draw needn't show every extreme that they name: `brick_count`: no device has more than 8 active bricks, and the counts of the two devices whose region indices differ by 4 / 2 (same sub and lane) sum to at most 8; some device has exactly 8. `brick_list`: each device's list holds distinct slot numbers; entries at or after the device's count are not live.
All inputs are finite; a program needn't handle non-finite values. No bound on the sum of `occupancy` on one device may be relied on, other than what follows from the above.
Results may differ from a plain program's by a relative error of at most 0.006.
Values may be sent and summed in bfloat16 or wider, within the bound.
A program may use at most 64 MiB of HBM per device.

v0:
```python
import jax
import jax.numpy as jnp
from jax import lax
from jax.sharding import PartitionSpec as P


def extended(value, sides, width):
    for axis, dim in sides:
        size, length = (lax.axis_size(axis), value.shape[dim])
        up = [(i, (i + 1) % size) for i in range(size - 1)]
        down = [(j, i) for i, j in up]
        last = lax.slice_in_dim(value, length - width, length, axis=dim)
        first = lax.slice_in_dim(value, 0, width, axis=dim)
        before = lax.ppermute(last, axis, up)
        after = lax.ppermute(first, axis, down)
        value = jnp.concatenate([before, value, after], axis=dim)
    return value


def body(
    features,
    occupancy,
    brick_list,
    brick_count,
    weight_one,
    scale_one,
    shift_one,
    weight_two,
    scale_two,
    shift_two,
):
    chans = features.shape[0]
    y_len = features.shape[2]
    z_len = features.shape[3]
    bricks_y = y_len // 8
    bricks_z = z_len // 8
    slot_total = bricks_y * bricks_z
    entries = brick_list.reshape(-1)
    capacity = entries.shape[0]
    count = brick_count.reshape(())
    valid = jnp.arange(capacity, dtype=jnp.int32) < count
    slot_live = jnp.any(
        (entries[:, None] == jnp.arange(slot_total, dtype=jnp.int32)[None, :]) & valid[:, None],
        axis=0,
    )
    brick_grid = slot_live.reshape(bricks_y, bricks_z)
    voxel_live = jnp.repeat(jnp.repeat(brick_grid, 8, 0), 8, 1)
    active = ((occupancy == 1) & voxel_live[None]).astype(jnp.bfloat16)
    active_float = active.astype(jnp.float32)[None]
    start = features * active[None]

    def dense_layer(padded, weight, scale, shift):
        kernel = weight.reshape(3, 3, 3, chans, chans).transpose(3, 4, 0, 1, 2)
        summed = lax.conv_general_dilated(
            padded[None], kernel, (1, 1, 1), "VALID", preferred_element_type=jnp.float32
        )[0]
        normed = jax.nn.relu(summed * scale[:, None, None, None] + shift[:, None, None, None])
        return (normed * active_float).astype(jnp.bfloat16)

    def layer(field, weight, scale, shift):
        padded = extended(field, (("region", 3), ("sub", 1), ("lane", 2)), 1)
        return dense_layer(padded, weight, scale, shift)

    first = layer(start, weight_one, scale_one, shift_one)
    second = layer(first, weight_two, scale_two, shift_two)
    summed = (second.astype(jnp.float32) + start.astype(jnp.float32)) * active_float
    return summed.astype(jnp.bfloat16)


def solution(mesh):
    placed = (
        P(None, "sub", "lane", ("groups", "region")),
        P("sub", "lane", ("groups", "region")),
        P(("groups", "region"), "sub", "lane", None),
        P(("groups", "region"), "sub", "lane"),
        P(),
        P(),
        P(),
        P(),
        P(),
        P(),
    )
    return jax.shard_map(
        body,
        mesh=mesh,
        in_specs=placed,
        out_specs=P(None, "sub", "lane", ("groups", "region")),
        check_vma=False,
    )
```

profile of v0, /device:TPU:0, one launch (start us, length us, event | category | flops | bytes accessed | tf_op | source)
XLA Modules:
  0.0 144.1 jit_solution(18221626263817037061)
XLA Ops:
  0.0 0.0 copy-start
  0.7 0.7 fusion.31
  1.5 0.1 broadcast_in_dim.8
  1.5 0.1 broadcast_in_dim.9
  1.6 0.8 fusion.38
  2.4 1.1 broadcast_multiply_fusion
  3.5 0.2 fusion.42
  3.7 5.0 %collective-permute-start = (bf16[32,8,8,1]{3,2,1,0:T(8,128)(2,1)S(1)}, bf16[32,8,8,1]{3,2,1,0:T(8,128)(2,1)S(1)}, u32[]{:S(2)}, u32[]{:S(2)}) collective-permute-start(bf16[32,8,8,1]{3,2,1,0:T(8,128)(2,1)S(1)} %get-tuple-element.17), channel_id=1, source_target_pairs={{0,4},{4,8},{8,12},{1,5},{5,9},{9,13},{2,6},{6,10},{10,14},{3,7},{... | collective-permute-start | bytes 12296 | tf_op jit(solution)/shard_map/ppermute | solution.py:14
  8.7 1.3 collective-permute-start.1
  10.0 9.8 %collective-permute-done = bf16[32,8,8,1]{3,2,1,0:T(8,128)(2,1)S(1)} collective-permute-done((bf16[32,8,8,1]{3,2,1,0:T(8,128)(2,1)S(1)}, bf16[32,8,8,1]{3,2,1,0:T(8,128)(2,1)S(1)}, u32[]{:S(2)}, u32[]{:S(2)}) %collective-permute-start) | collective-permute-done | bytes 4128 | tf_op jit(solution)/shard_map/ppermute | solution.py:14
  19.8 4.1 %collective-permute-done.1 = bf16[32,8,8,1]{3,2,1,0:T(8,128)(2,1)S(1)} collective-permute-done((bf16[32,8,8,1]{3,2,1,0:T(8,128)(2,1)S(1)}, bf16[32,8,8,1]{3,2,1,0:T(8,128)(2,1)S(1)}, u32[]{:S(2)}, u32[]{:S(2)}) %collective-permute-start.1) | collective-permute-done | bytes 4128 | tf_op jit(solution)/shard_map/ppermute | solution.py:15
  24.0 0.2 pad_maximum_fusion.7
  24.2 3.4 %collective-permute-start.2 = (bf16[32,1,8,130]{3,2,1,0:T(8,128)(2,1)S(1)}, bf16[32,1,8,130]{3,2,1,0:T(8,128)(2,1)S(1)}, u32[]{:S(2)}, u32[]{:S(2)}) collective-permute-start(bf16[32,1,8,130]{3,2,1,0:T(8,128)(2,1)S(1)} %get-tuple-element.9), channel_id=1, source_target_pairs={{0,2},{1,3},{4,6},{5,7},{8,10},{9,11},{12,14},{13,15},{16,18},{17,... | collective-permute-start | bytes 199688 | tf_op jit(solution)/shard_map/ppermute | solution.py:14
  27.6 1.3 collective-permute-start.3
  28.9 1.2 collective-permute-done.2
  30.1 4.4 %collective-permute-done.3 = bf16[32,1,8,130]{3,2,1,0:T(8,128)(2,1)S(1)} collective-permute-done((bf16[32,1,8,130]{3,2,1,0:T(8,128)(2,1)S(1)}, bf16[32,1,8,130]{3,2,1,0:T(8,128)(2,1)S(1)}, u32[]{:S(2)}, u32[]{:S(2)}) %collective-permute-start.3) | collective-permute-done | bytes 66592 | tf_op jit(solution)/shard_map/ppermute | solution.py:15
  34.4 0.7 pad_maximum_fusion
  35.1 0.4 copy.67
  35.6 1.3 collective-permute-start.4
  36.9 1.5 %collective-permute-start.5 = (bf16[32,10,1,130]{3,0,2,1:T(8,128)(2,1)S(1)}, bf16[32,10,1,130]{3,0,2,1:T(8,128)(2,1)S(1)}, u32[]{:S(2)}, u32[]{:S(2)}) collective-permute-start(bf16[32,10,1,130]{3,0,2,1:T(8,128)(2,1)S(1)} %get-tuple-element.14), channel_id=1, source_target_pairs={{1,0},{3,2},{5,4},{7,6},{9,8},{11,10},{13,12},{15,14},{17,16},{19,... | collective-permute-start | bytes 249608 | tf_op jit(solution)/shard_map/ppermute | solution.py:15
  38.4 0.0 collective-permute-done.4
  38.4 1.8 %collective-permute-done.5 = bf16[32,10,1,130]{3,0,2,1:T(8,128)(2,1)S(1)} collective-permute-done((bf16[32,10,1,130]{3,0,2,1:T(8,128)(2,1)S(1)}, bf16[32,10,1,130]{3,0,2,1:T(8,128)(2,1)S(1)}, u32[]{:S(2)}, u32[]{:S(2)}) %collective-permute-start.5) | collective-permute-done | bytes 83232 | tf_op jit(solution)/shard_map/ppermute | solution.py:15
  40.2 0.3 maximum_bitcast_fusion
  40.5 0.4 pad
  40.9 6.0 %reshape.28 = bf16[32,10,10,1,8,17]{5,4,0,2,1,3:T(8,128)(2,1)} reshape(bf16[32,10,10,1,136]{4,0,2,1,3:T(8,128)(2,1)S(1)} %pad) | data formatting | bytes 1740800 | tf_op jit(solution)/shard_map/conv_general_dilated | solution.py:54
  47.0 10.2 %copy.71 = bf16[32,10,10,1,8,17]{0,4,5,2,1,3:T(8,128)(2,1)} copy(bf16[32,10,10,1,8,17]{5,4,0,2,1,3:T(8,128)(2,1)} %reshape.28) | data formatting | bytes 1740800 | tf_op jit(solution)/shard_map/conv_general_dilated | solution.py:54
  57.2 1.1 slice.56
  58.3 0.0 copy-done
  58.3 0.0 copy-done.8
  58.3 9.9 %broadcast_select_fusion.1 = f32[8,8,8,17,32]{4,2,3,1,0:T(8,128)S(1)} fusion(pred[8,17]{0,1:T(8,128)(4,1)S(1)} %copy-done.8, bf16[3,3,3,32,32]{4,3,2,1,0:T(8,128)(2,1)S(1)} %bitcast.57, bf16[32,10,10,1,7,2]{0,4,5,2,1,3:T(8,128)(2,1)S(1)} %slice.56, bf16[32,10,10,1,8,17]{0,4,5,2,1,3:T(8,128)(2,1)} %copy.71), kind=kOutput, calls=%fused_computation.16 | convolution fusion | flops 484493312 | bytes 2129544 | tf_op jit(solution)/shard_map/conv_general_dilated | solution.py:54
  68.2 0.8 copy.72
  69.0 2.2 %slice.57 = f32[8,8,1,128,32]{4,1,3,0,2:T(8,128)} slice(f32[8,8,1,136,32]{4,1,3,0,2:T(8,128)S(1)} %bitcast.58), slice={[0:8], [0:8], [0:1], [0:128], [0:32]} | slice | bytes 2097152 | tf_op jit(solution)/shard_map/conv_general_dilated | solution.py:54
  71.2 3.2 %copy.81 = f32[8,8,1,128,32]{3,1,0,4,2:T(8,128)S(1)} copy(f32[8,8,1,128,32]{4,1,3,0,2:T(8,128)} %slice.57) | data formatting | bytes 2097152
  74.4 0.0 copy-done.3
  74.5 0.0 copy-done.4
  74.5 0.2 fusion.29
  74.7 0.2 fusion.41
  75.0 3.5 %collective-permute-start.6 = (bf16[32,8,8,1]{3,2,1,0:T(8,128)(2,1)S(1)}, bf16[32,8,8,1]{3,2,1,0:T(8,128)(2,1)S(1)}, u32[]{:S(2)}, u32[]{:S(2)}) collective-permute-start(bf16[32,8,8,1]{3,2,1,0:T(8,128)(2,1)S(1)} %get-tuple-element.15), channel_id=1, source_target_pairs={{0,4},{4,8},{8,12},{1,5},{5,9},{9,13},{2,6},{6,10},{10,14},{3,7},{... | collective-permute-start | bytes 12296 | tf_op jit(solution)/shard_map/ppermute | solution.py:14
  78.5 1.3 collective-permute-start.7
  79.8 10.1 %collective-permute-done.6 = bf16[32,8,8,1]{3,2,1,0:T(8,128)(2,1)S(1)} collective-permute-done((bf16[32,8,8,1]{3,2,1,0:T(8,128)(2,1)S(1)}, bf16[32,8,8,1]{3,2,1,0:T(8,128)(2,1)S(1)}, u32[]{:S(2)}, u32[]{:S(2)}) %collective-permute-start.6) | collective-permute-done | bytes 4128 | tf_op jit(solution)/shard_map/ppermute | solution.py:14
  89.9 4.1 %collective-permute-done.7 = bf16[32,8,8,1]{3,2,1,0:T(8,128)(2,1)S(1)} collective-permute-done((bf16[32,8,8,1]{3,2,1,0:T(8,128)(2,1)S(1)}, bf16[32,8,8,1]{3,2,1,0:T(8,128)(2,1)S(1)}, u32[]{:S(2)}, u32[]{:S(2)}) %collective-permute-start.7) | collective-permute-done | bytes 4128 | tf_op jit(solution)/shard_map/ppermute | solution.py:15
  94.1 0.2 pad_maximum_fusion.4
  94.2 1.7 %collective-permute-start.8 = (bf16[32,1,8,130]{3,2,1,0:T(8,128)(2,1)S(1)}, bf16[32,1,8,130]{3,2,1,0:T(8,128)(2,1)S(1)}, u32[]{:S(2)}, u32[]{:S(2)}) collective-permute-start(bf16[32,1,8,130]{3,2,1,0:T(8,128)(2,1)S(1)} %get-tuple-element.7), channel_id=1, source_target_pairs={{0,2},{1,3},{4,6},{5,7},{8,10},{9,11},{12,14},{13,15},{16,18},{17,... | collective-permute-start | bytes 199688 | tf_op jit(solution)/shard_map/ppermute | solution.py:14
  96.0 1.3 collective-permute-start.9
  97.3 1.0 collective-permute-done.8
  98.2 4.6 %collective-permute-done.9 = bf16[32,1,8,130]{3,2,1,0:T(8,128)(2,1)S(1)} collective-permute-done((bf16[32,1,8,130]{3,2,1,0:T(8,128)(2,1)S(1)}, bf16[32,1,8,130]{3,2,1,0:T(8,128)(2,1)S(1)}, u32[]{:S(2)}, u32[]{:S(2)}) %collective-permute-start.9) | collective-permute-done | bytes 66592 | tf_op jit(solution)/shard_map/ppermute | solution.py:15
  102.8 0.7 pad_maximum_fusion.1
  103.5 0.4 copy.74
  104.0 1.3 collective-permute-start.10
  105.3 1.3 collective-permute-start.11
  106.6 0.0 collective-permute-done.10
  106.6 2.0 %collective-permute-done.11 = bf16[32,10,1,130]{3,0,2,1:T(8,128)(2,1)S(1)} collective-permute-done((bf16[32,10,1,130]{3,0,2,1:T(8,128)(2,1)S(1)}, bf16[32,10,1,130]{3,0,2,1:T(8,128)(2,1)S(1)}, u32[]{:S(2)}, u32[]{:S(2)}) %collective-permute-start.11) | collective-permute-done | bytes 83232 | tf_op jit(solution)/shard_map/ppermute | solution.py:15
  108.6 0.3 maximum_bitcast_fusion.1
  108.9 0.4 pad.2
  109.3 6.0 %reshape.35 = bf16[32,10,10,1,8,17]{5,4,0,2,1,3:T(8,128)(2,1)} reshape(bf16[32,10,10,1,136]{4,0,2,1,3:T(8,128)(2,1)S(1)} %pad.2) | data formatting | bytes 1740800 | tf_op jit(solution)/shard_map/conv_general_dilated | solution.py:54
  115.4 10.2 %copy.78 = bf16[32,10,10,1,8,17]{0,4,5,2,1,3:T(8,128)(2,1)} copy(bf16[32,10,10,1,8,17]{5,4,0,2,1,3:T(8,128)(2,1)} %reshape.35) | data formatting | bytes 1740800 | tf_op jit(solution)/shard_map/conv_general_dilated | solution.py:54
  125.6 1.1 slice.62
  126.7 9.9 %broadcast_select_fusion = f32[8,8,8,17,32]{4,2,3,1,0:T(8,128)S(1)} fusion(pred[8,17]{0,1:T(8,128)(4,1)S(1)} %copy-done.8, bf16[3,3,3,32,32]{4,3,2,1,0:T(8,128)(2,1)S(1)} %bitcast.60, bf16[32,10,10,1,7,2]{0,4,5,2,1,3:T(8,128)(2,1)S(1)} %slice.62, bf16[32,10,10,1,8,17]{0,4,5,2,1,3:T(8,128)(2,1)} %copy.78), kind=kOutput, calls=%fused_computation.15 | convolution fusion | flops 484493312 | bytes 2129544 | tf_op jit(solution)/shard_map/conv_general_dilated | solution.py:54
  136.6 0.8 copy.79
  137.4 0.0 copy-start.1
  137.4 2.2 %slice.63 = f32[8,8,1,128,32]{4,1,3,0,2:T(8,128)} slice(f32[8,8,1,136,32]{4,1,3,0,2:T(8,128)S(1)} %bitcast.59), slice={[0:8], [0:8], [0:1], [0:128], [0:32]} | slice | bytes 2097152 | tf_op jit(solution)/shard_map/conv_general_dilated | solution.py:54
  139.6 3.3 %copy.82 = f32[8,8,1,128,32]{3,1,0,4,2:T(8,128)S(1)} copy(f32[8,8,1,128,32]{4,1,3,0,2:T(8,128)} %slice.63) | data formatting | bytes 2097152
  142.9 1.2 multiply_convert_fusion
  144.1 0.0 copy-done.1
  (14 shorter events, 0.1 us)
Async XLA Ops:
  0.0 58.3 %copy-start = (bf16[27,32,32]{2,1,0:T(8,128)(2,1)S(1)}, bf16[27,32,32]{2,1,0:T(8,128)(2,1)}, u32[]{:S(2)}) copy-start(bf16[27,32,32]{2,1,0:T(8,128)(2,1)} %param.14) | copy-start | bytes 165892
  3.7 16.1 %collective-permute-start = (bf16[32,8,8,1]{3,2,1,0:T(8,128)(2,1)S(1)}, bf16[32,8,8,1]{3,2,1,0:T(8,128)(2,1)S(1)}, u32[]{:S(2)}, u32[]{:S(2)}) collective-permute-start(bf16[32,8,8,1]{3,2,1,0:T(8,128)(2,1)S(1)} %get-tuple-element.17), channel_id=1, source_target_pairs={{0,4},{4,8},{8,12},{1,5},{5,9},{9,13},{2,6},{6,10},{10,14},{3,7},{... | collective-permute-start | bytes 12296 | tf_op jit(solution)/shard_map/ppermute | solution.py:14
  8.7 15.3 %collective-permute-start.1 = (bf16[32,8,8,1]{3,2,1,0:T(8,128)(2,1)S(1)}, bf16[32,8,8,1]{3,2,1,0:T(8,128)(2,1)S(1)}, u32[]{:S(2)}, u32[]{:S(2)}) collective-permute-start(bf16[32,8,8,1]{3,2,1,0:T(8,128)(2,1)S(1)} %get-tuple-element.18), channel_id=1, source_target_pairs={{4,0},{8,4},{12,8},{5,1},{9,5},{13,9},{6,2},{10,6},{14,10},{7,3},{... | collective-permute-start | bytes 12296 | tf_op jit(solution)/shard_map/ppermute | solution.py:15
  24.2 5.9 %collective-permute-start.2 = (bf16[32,1,8,130]{3,2,1,0:T(8,128)(2,1)S(1)}, bf16[32,1,8,130]{3,2,1,0:T(8,128)(2,1)S(1)}, u32[]{:S(2)}, u32[]{:S(2)}) collective-permute-start(bf16[32,1,8,130]{3,2,1,0:T(8,128)(2,1)S(1)} %get-tuple-element.9), channel_id=1, source_target_pairs={{0,2},{1,3},{4,6},{5,7},{8,10},{9,11},{12,14},{13,15},{16,18},{17,... | collective-permute-start | bytes 199688 | tf_op jit(solution)/shard_map/ppermute | solution.py:14
  27.6 6.9 %collective-permute-start.3 = (bf16[32,1,8,130]{3,2,1,0:T(8,128)(2,1)S(1)}, bf16[32,1,8,130]{3,2,1,0:T(8,128)(2,1)S(1)}, u32[]{:S(2)}, u32[]{:S(2)}) collective-permute-start(bf16[32,1,8,130]{3,2,1,0:T(8,128)(2,1)S(1)} %get-tuple-element.10), channel_id=1, source_target_pairs={{2,0},{3,1},{6,4},{7,5},{10,8},{11,9},{14,12},{15,13},{18,16},{19,... | collective-permute-start | bytes 199688 | tf_op jit(solution)/shard_map/ppermute | solution.py:15
  35.6 2.8 %collective-permute-start.4 = (bf16[32,10,1,130]{3,0,2,1:T(8,128)(2,1)S(1)}, bf16[32,10,1,130]{3,0,2,1:T(8,128)(2,1)S(1)}, u32[]{:S(2)}, u32[]{:S(2)}) collective-permute-start(bf16[32,10,1,130]{3,0,2,1:T(8,128)(2,1)S(1)} %get-tuple-element.13), channel_id=1, source_target_pairs={{0,1},{2,3},{4,5},{6,7},{8,9},{10,11},{12,13},{14,15},{16,17},{18,... | collective-permute-start | bytes 249608 | tf_op jit(solution)/shard_map/ppermute | solution.py:14
  36.9 3.3 %collective-permute-start.5 = (bf16[32,10,1,130]{3,0,2,1:T(8,128)(2,1)S(1)}, bf16[32,10,1,130]{3,0,2,1:T(8,128)(2,1)S(1)}, u32[]{:S(2)}, u32[]{:S(2)}) collective-permute-start(bf16[32,10,1,130]{3,0,2,1:T(8,128)(2,1)S(1)} %get-tuple-element.14), channel_id=1, source_target_pairs={{1,0},{3,2},{5,4},{7,6},{9,8},{11,10},{13,12},{15,14},{17,16},{19,... | collective-permute-start | bytes 249608 | tf_op jit(solution)/shard_map/ppermute | solution.py:15
  47.0 11.3 %copy-start.8 = (pred[8,17]{0,1:T(8,128)(4,1)S(1)}, pred[8,17]{0,1:T(8,128)(4,1)}, u32[]{:S(2)}) copy-start(pred[8,17]{0,1:T(8,128)(4,1)} %constant.18) | copy-start | bytes 412
  71.2 3.2 %copy-start.3 = (f32[32]{0:T(128)S(1)}, f32[32]{0:T(128)}, u32[]{:S(2)}) copy-start(f32[32]{0:T(128)} %param.16) | copy-start | bytes 388
  71.2 3.2 %copy-start.4 = (f32[32]{0:T(128)S(1)}, f32[32]{0:T(128)}, u32[]{:S(2)}) copy-start(f32[32]{0:T(128)} %param.15) | copy-start | bytes 388
  75.0 14.9 %collective-permute-start.6 = (bf16[32,8,8,1]{3,2,1,0:T(8,128)(2,1)S(1)}, bf16[32,8,8,1]{3,2,1,0:T(8,128)(2,1)S(1)}, u32[]{:S(2)}, u32[]{:S(2)}) collective-permute-start(bf16[32,8,8,1]{3,2,1,0:T(8,128)(2,1)S(1)} %get-tuple-element.15), channel_id=1, source_target_pairs={{0,4},{4,8},{8,12},{1,5},{5,9},{9,13},{2,6},{6,10},{10,14},{3,7},{... | collective-permute-start | bytes 12296 | tf_op jit(solution)/shard_map/ppermute | solution.py:14
  78.5 15.6 %collective-permute-start.7 = (bf16[32,8,8,1]{3,2,1,0:T(8,128)(2,1)S(1)}, bf16[32,8,8,1]{3,2,1,0:T(8,128)(2,1)S(1)}, u32[]{:S(2)}, u32[]{:S(2)}) collective-permute-start(bf16[32,8,8,1]{3,2,1,0:T(8,128)(2,1)S(1)} %get-tuple-element.16), channel_id=1, source_target_pairs={{4,0},{8,4},{12,8},{5,1},{9,5},{13,9},{6,2},{10,6},{14,10},{7,3},{... | collective-permute-start | bytes 12296 | tf_op jit(solution)/shard_map/ppermute | solution.py:15
  94.2 4.0 %collective-permute-start.8 = (bf16[32,1,8,130]{3,2,1,0:T(8,128)(2,1)S(1)}, bf16[32,1,8,130]{3,2,1,0:T(8,128)(2,1)S(1)}, u32[]{:S(2)}, u32[]{:S(2)}) collective-permute-start(bf16[32,1,8,130]{3,2,1,0:T(8,128)(2,1)S(1)} %get-tuple-element.7), channel_id=1, source_target_pairs={{0,2},{1,3},{4,6},{5,7},{8,10},{9,11},{12,14},{13,15},{16,18},{17,... | collective-permute-start | bytes 199688 | tf_op jit(solution)/shard_map/ppermute | solution.py:14
  96.0 6.9 %collective-permute-start.9 = (bf16[32,1,8,130]{3,2,1,0:T(8,128)(2,1)S(1)}, bf16[32,1,8,130]{3,2,1,0:T(8,128)(2,1)S(1)}, u32[]{:S(2)}, u32[]{:S(2)}) collective-permute-start(bf16[32,1,8,130]{3,2,1,0:T(8,128)(2,1)S(1)} %get-tuple-element.8), channel_id=1, source_target_pairs={{2,0},{3,1},{6,4},{7,5},{10,8},{11,9},{14,12},{15,13},{18,16},{19,... | collective-permute-start | bytes 199688 | tf_op jit(solution)/shard_map/ppermute | solution.py:15
  104.0 2.6 %collective-permute-start.10 = (bf16[32,10,1,130]{3,0,2,1:T(8,128)(2,1)S(1)}, bf16[32,10,1,130]{3,0,2,1:T(8,128)(2,1)S(1)}, u32[]{:S(2)}, u32[]{:S(2)}) collective-permute-start(bf16[32,10,1,130]{3,0,2,1:T(8,128)(2,1)S(1)} %get-tuple-element.11), channel_id=1, source_target_pairs={{0,1},{2,3},{4,5},{6,7},{8,9},{10,11},{12,13},{14,15},{16,17},{18,... | collective-permute-start | bytes 249608 | tf_op jit(solution)/shard_map/ppermute | solution.py:14
  105.3 3.3 %collective-permute-start.11 = (bf16[32,10,1,130]{3,0,2,1:T(8,128)(2,1)S(1)}, bf16[32,10,1,130]{3,0,2,1:T(8,128)(2,1)S(1)}, u32[]{:S(2)}, u32[]{:S(2)}) collective-permute-start(bf16[32,10,1,130]{3,0,2,1:T(8,128)(2,1)S(1)} %get-tuple-element.12), channel_id=1, source_target_pairs={{1,0},{3,2},{5,4},{7,6},{9,8},{11,10},{13,12},{15,14},{17,16},{19,... | collective-permute-start | bytes 249608 | tf_op jit(solution)/shard_map/ppermute | solution.py:15
  115.4 11.3 %copy-start.7 = (bf16[27,32,32]{2,1,0:T(8,128)(2,1)S(1)}, bf16[27,32,32]{2,1,0:T(8,128)(2,1)}, u32[]{:S(2)}) copy-start(bf16[27,32,32]{2,1,0:T(8,128)(2,1)} %param.17) | copy-start | bytes 165892
  137.4 6.7 %copy-start.1 = (bf16[27,32,32]{2,1,0:T(8,128)(2,1)S(1)}, bf16[27,32,32]{2,1,0:T(8,128)(2,1)}, u32[]{:S(2)}) copy-start(bf16[27,32,32]{2,1,0:T(8,128)(2,1)} %param.14) | copy-start | bytes 165892
  139.6 3.3 %copy-start.2 = (bf16[32,8,8,128]{3,2,1,0:T(8,128)(2,1)S(1)}, bf16[32,8,8,128]{3,2,1,0:T(8,128)(2,1)}, u32[]{:S(2)}) copy-start(bf16[32,8,8,128]{3,2,1,0:T(8,128)(2,1)} %param.10) | copy-start | bytes 1572868
  139.6 3.3 %copy-start.5 = (f32[32]{0:T(128)S(1)}, f32[32]{0:T(128)}, u32[]{:S(2)}) copy-start(f32[32]{0:T(128)} %param.19) | copy-start | bytes 388
  139.6 3.3 %copy-start.6 = (f32[32]{0:T(128)S(1)}, f32[32]{0:T(128)}, u32[]{:S(2)}) copy-start(f32[32]{0:T(128)} %param.18) | copy-start | bytes 388
where the time goes:
time: 145 us; the launch traced here: 144 us
  local copies, waits for them, and re-layouts  49.7 us (34%)
  waiting for transfers between devices  43.2 us (30%)
  starting transfers between devices  24.1 us (17%)
  matrix products  19.7 us (14%)
  other arithmetic  6.34 us (4%)
    conv_general_dilated x10, local copies, waits for them, and re-layouts, dense_layer(): lax.conv_general_dilated(padded[None], kernel, (1, 1, 1), 'VALID', prefer...  40.7 us
    ppermute x6, waiting for transfers between devices, extended(): before = lax.ppermute(last, axis, up)  22.2 us
    ppermute x6, waiting for transfers between devices, extended(): after = lax.ppermute(first, axis, down)  21 us
    conv_general_dilated x2, matrix products, dense_layer(): lax.conv_general_dilated(padded[None], kernel, (1, 1, 1), 'VALID', prefer...  19.7 us
    ppermute x6, starting transfers between devices, extended(): before = lax.ppermute(last, axis, up)  16.2 us
    ppermute x6, starting transfers between devices, extended(): after = lax.ppermute(first, axis, down)  7.93 us
    unnamed x20, local copies, waits for them, and re-layouts  6.52 us
  transfers between devices with their start and end apart: 12, of which 10 were waited for; matrix products, arithmetic and copies ran while one was open for 0% of the time, Pallas kernels for 0%

commit v1 on v0

v1 whole, which is shorter than its diff:
```python
import functools

import jax
import jax.numpy as jnp
from jax import lax
from jax.experimental import pallas as pl
from jax.experimental.pallas import tpu as pltpu
from jax.sharding import PartitionSpec as P

BF = jnp.bfloat16
F32 = jnp.float32
MESH = pl.DeviceIdType.MESH

KINDS = [
    (dr, ds, dl) for dr in (0, -1, 1) for ds in (0, -1, 1) for dl in (0, 1) if (dr, ds, dl) != (0, 0, 0)
]


def dot(a, b):
    return jnp.dot(a, b, preferred_element_type=F32)


def dot_nt(a, b):
    return lax.dot_general(a, b, (((1,), (1,)), ((), ())), preferred_element_type=F32)


def iota(shape, dim):
    return lax.broadcasted_iota(jnp.int32, shape, dim)


def onehot(cond):
    return jnp.where(cond, 1.0, 0.0).astype(BF)


def kernel(
    n_region, n_sub,
    feat, occ, bricks, count, w1, s1, h1, w2, s2, h2, out,
    D, DY, B, BY, BC, WC, ACC, G, ACT, SX, SY, SZ, RX, RY, RZ, send_sem, recv_sem,
):
    r = lax.axis_index("region")
    s = lax.axis_index("sub")
    l = lax.axis_index("lane")
    edge = 7 * (1 - l)
    far = 7 * l

    def inside(dr, ds):
        a, b = r + dr, s + ds
        return (a >= 0) & (a < n_region) & (b >= 0) & (b < n_sub)

    def target(dr, ds, dl):
        return {"region": r + dr, "sub": s + ds, "lane": 1 - l if dl else l}

    barrier = pltpu.get_barrier_semaphore()
    RX[...] = jnp.zeros_like(RX)
    RY[...] = jnp.zeros_like(RY)
    RZ[...] = jnp.zeros_like(RZ)
    for kind in KINDS:
        @pl.when(inside(kind[0], kind[1]))
        def _(kind=kind):
            pl.semaphore_signal(barrier, inc=1, device_id=target(*kind), device_id_type=MESH)

    def message(rnd, k):
        dr, ds, dl = KINDS[k]
        if dr:
            src = SZ.at[rnd]
            dst = RZ.at[rnd, dl, pl.ds((0 if dr == 1 else 48) + (1 - ds) * 16, 16)]
        elif not dl:
            src = SX.at[rnd, 0 if ds == -1 else 1]
            dst = RX.at[rnd, 1 if ds == -1 else 0]
        elif ds == 0:
            src = SY.at[rnd]
            dst = RY.at[rnd, pl.ds(32, 256)]
        else:
            src = SY.at[rnd, pl.ds(0 if ds == -1 else 224, 32)]
            dst = RY.at[rnd, pl.ds(288 if ds == -1 else 0, 32)]
        return pltpu.make_async_remote_copy(
            src_ref=src, dst_ref=dst, send_sem=send_sem.at[rnd, k], recv_sem=recv_sem.at[rnd, k],
            device_id=target(dr, ds, dl), device_id_type=MESH,
        )

    def send(rnd):
        for k, (dr, ds, dl) in enumerate(KINDS):
            @pl.when(inside(dr, ds))
            def _(k=k):
                message(rnd, k).start()

    def arrived(rnd):
        for k, (dr, ds, dl) in enumerate(KINDS):
            @pl.when(inside(-dr, -ds))
            def _(k=k):
                message(rnd, k).wait_recv()

    def sent(rnd):
        for k, (dr, ds, dl) in enumerate(KINDS):
            @pl.when(inside(dr, ds))
            def _(k=k):
                message(rnd, k).wait_send()

    lane128 = iota((8, 128), 1)
    slot = lane128 >> 3
    live = jnp.zeros((8, 128), F32)
    n_live = count[0, 0, 0]
    for k in range(bricks.shape[3]):
        entry = jnp.where(k < n_live, bricks[0, 0, 0, k], -1)
        live = jnp.where(slot == entry, 1.0, live)
    for x in range(8):
        ACT[x] = jnp.where(occ[x] == 1, live, 0.0)

    zl = iota((256, 128), 1)

    def shifted(v):
        before = jnp.where(zl[: v.shape[0]] == 0, 0.0, pltpu.roll(v, 1, 1))
        after = jnp.where(zl[: v.shape[0]] == 127, 0.0, pltpu.roll(v, 127, 1))
        return before.astype(BF), v.astype(BF), after.astype(BF)

    def places(x):
        got = []
        if -1 <= x <= 4:
            got.append((x + 1, 0))
        if 3 <= x <= 8:
            got.append((x - 3, 1))
        return got

    def put_plane(rnd, x, v):
        three = shifted(v)
        for p, h in places(x):
            for dz in range(3):
                D[rnd, p, dz, :, pl.ds(h * 128, 128)] = three[dz]
        if x == 0:
            SX[rnd, 0] = three[1]
        if x == 7:
            SX[rnd, 1] = three[1]

    ci = iota((32, 256), 0)
    cj = iota((32, 256), 1)
    spread = onehot(ci == (cj >> 3))
    pick_edge = onehot((ci == (cj >> 3)) & ((cj & 7) == edge))
    e_row = iota((16, 128), 0)
    e_lane = iota((16, 128), 1)

    def pack(rnd):
        columns = jnp.zeros((16, 256), F32)
        for x in range(8):
            p, h = places(x)[0]
            take = onehot(((e_row == x) & (e_lane == 0)) | ((e_row == 8 + x) & (e_lane == 127)))
            v = D[rnd, p, 1, :, pl.ds(h * 128, 128)]
            columns += dot_nt(take, v)
            SY[rnd, pl.ds(x * 32, 32)] = dot(pick_edge, v).astype(BF)
        SZ[rnd] = columns.astype(BF)

    for x in range(8):
        v = feat[:, x].astype(F32) * ACT[x][None]
        put_plane(0, x, v.reshape(256, 128))
    pack(0)
    def span(at, size):
        return 1 + jnp.where(at > 0, 1, 0) + jnp.where(at < size - 1, 1, 0)

    pl.semaphore_wait(barrier, span(r, n_region) * span(s, n_sub) * 2 - 1)
    send(0)

    ri = iota((256, 256), 0)
    rj = iota((256, 256), 1)
    order = onehot((ri >> 3 == (rj & 31)) & ((ri & 7) == (rj >> 5)))
    bi = iota((256, 32), 0)
    bj = iota((256, 32), 1)
    put_edge = onehot(((bi >> 3) == bj) & ((bi & 7) == edge))
    band = [onehot((cj & 7) == k) for k in range(8)]
    far_band = onehot((cj & 7) == far)

    def build(layer, w):
        WC[...] = dot(w[...].reshape(27 * 32, 32), spread).astype(BF)
        for dx in range(3):
            for dz in range(3):
                taps = [WC[pl.ds((9 * dx + 3 * dy + dz) * 32, 32)] for dy in range(3)]
                blocks = []
                for y in range(8):
                    block = taps[1] * band[y]
                    if y > 0:
                        block = block + taps[0] * band[y - 1]
                    if y < 7:
                        block = block + taps[2] * band[y + 1]
                    blocks.append(block)
                full = jnp.concatenate(blocks, axis=0)
                B[layer, :, pl.ds((dx * 3 + dz) * 256, 256)] = dot(order, full).astype(BF)
                if dz != 1:
                    start = pl.multiple_of((9 * dx + 3 * (2 - 2 * l) + dz) * 32, 32)
                    BC[layer, dx * 2 + dz // 2] = dot(put_edge, WC[pl.ds(start, 32)] * far_band).astype(BF)
        side = jnp.zeros((32, 288), F32)
        pi = iota((32, 288), 0)
        pj = iota((32, 288), 1)
        for dx in range(3):
            for dz in range(3):
                tap = w[9 * dx + 3 * (2 - 2 * l) + dz]
                side += dot(tap, onehot(pj == pi + 32 * (dx * 3 + dz)))
        BY[layer] = dot(put_edge, side.astype(BF)).astype(BF)

    build(0, w1)
    build(1, w2)

    si = iota((96, 96), 0)
    sj = iota((96, 96), 1)
    q, j = si >> 4, si & 15
    plus = q & 1
    e = (j >> 1) + (q >> 1) + 7
    source = plus * 48 + (e >> 3) * 16 + (1 - plus) * 8 + (e & 7)
    place = onehot((sj == source) & ((j & 1) == 1 - plus))

    def rows_of(ref):
        own = jnp.broadcast_to(ref[...], (256, 32))
        return jnp.sum(jnp.where((bi >> 3) == bj, own, 0.0), axis=1, keepdims=True)

    G[...] = jnp.zeros_like(G)

    def main(layer, xx):
        return dot(B[layer], D[layer, pl.ds(xx, 3)].reshape(2304, 256))

    def layer_sums(layer):
        for xx in (1, 2):
            ACC[xx] = main(layer, xx)
        arrived(layer)
        for x, side in ((-1, 0), (8, 1)):
            put_plane(layer, x, RX[layer, side].astype(F32))
        for x in range(-1, 9):
            three = shifted(RY[layer, pl.ds((x + 1) * 32, 32)].astype(F32))
            for p, h in places(x):
                for dz in range(3):
                    DY[layer, pl.ds(p * 96 + dz * 32, 32), pl.ds(h * 128, 128)] = three[dz]
        own = dot(place, RZ[layer, 0]).astype(BF)
        other = dot(place, RZ[layer, 1]).astype(BF)
        total = jnp.zeros((256, 16), F32)
        for q in range(6):
            dx, dz = q // 2, 2 * (q % 2)
            total += dot_nt(B[layer, :, pl.ds((dx * 3 + dz) * 256, 256)], own[q * 16 : q * 16 + 16])
            total += dot_nt(BC[layer, q], other[q * 16 : q * 16 + 16])
        G[:, pl.ds(0, 16)] = total

    ends = (zl == 0) | (zl == 127)

    def finish(layer, xx, scale, shift):
        acc = ACC[xx] if xx in (1, 2) else main(layer, xx)
        acc = acc + dot(BY[layer], DY[layer, pl.ds(xx * 96, 288)])
        got = []
        for h in range(2):
            x = xx + 4 * h
            v = acc[:, h * 128 : h * 128 + 128]
            v = v + jnp.where(ends, pltpu.roll(G[...], 128 - (2 * x + 1), 1), 0.0)
            v = jnp.maximum(v * scale + shift, 0.0).reshape(32, 8, 128) * ACT[x][None]
            got.append((x, v))
        return got

    layer_sums(0)
    scale, shift = rows_of(s1), rows_of(h1)
    for xx in (0, 3, 1, 2):
        for x, v in finish(0, xx, scale, shift):
            put_plane(1, x, v.reshape(256, 128).astype(BF).astype(F32))
    pack(1)
    send(1)

    layer_sums(1)
    scale, shift = rows_of(s2), rows_of(h2)
    for xx in (1, 2, 0, 3):
        for x, v in finish(1, xx, scale, shift):
            p, h = places(x)[0]
            begin = D[0, p, 1, :, pl.ds(h * 128, 128)].astype(F32).reshape(32, 8, 128)
            v = (v.astype(BF).astype(F32) + begin) * ACT[x][None]
            out[:, x] = v.astype(BF)
    sent(0)
    sent(1)


def body(n_region, n_sub, features, occupancy, brick_list, brick_count, w1, s1, h1, w2, s2, h2):
    assert features.shape == (32, 8, 8, 128)
    vmem = pl.BlockSpec(memory_space=pltpu.VMEM)
    smem = pl.BlockSpec(memory_space=pltpu.SMEM)
    return pl.pallas_call(
        functools.partial(kernel, n_region, n_sub),
        out_shape=jax.ShapeDtypeStruct(features.shape, BF),
        in_specs=[vmem, vmem, smem, smem] + [vmem] * 6,
        out_specs=vmem,
        scratch_shapes=[
            pltpu.VMEM((2, 6, 3, 256, 256), BF),
            pltpu.VMEM((2, 576, 256), BF),
            pltpu.VMEM((2, 256, 2304), BF),
            pltpu.VMEM((2, 256, 288), BF),
            pltpu.VMEM((2, 6, 256, 256), BF),
            pltpu.VMEM((864, 256), BF),
            pltpu.VMEM((4, 256, 256), F32),
            pltpu.VMEM((256, 128), F32),
            pltpu.VMEM((8, 8, 128), F32),
            pltpu.VMEM((2, 2, 256, 128), BF),
            pltpu.VMEM((2, 256, 128), BF),
            pltpu.VMEM((2, 16, 256), BF),
            pltpu.VMEM((2, 2, 256, 128), BF),
            pltpu.VMEM((2, 320, 128), BF),
            pltpu.VMEM((2, 2, 96, 256), BF),
            pltpu.SemaphoreType.DMA((2, len(KINDS))),
            pltpu.SemaphoreType.DMA((2, len(KINDS))),
        ],
        compiler_params=pltpu.CompilerParams(
            collective_id=0, has_side_effects=True, vmem_limit_bytes=48 * 1024 * 1024
        ),
    )(features, occupancy, brick_list, brick_count, w1, s1.reshape(1, -1), h1.reshape(1, -1), w2, s2.reshape(1, -1), h2.reshape(1, -1))


def solution(mesh):
    assert mesh.shape["lane"] == 2
    placed = (
        P(None, "sub", "lane", ("groups", "region")),
        P("sub", "lane", ("groups", "region")),
        P(("groups", "region"), "sub", "lane", None),
        P(("groups", "region"), "sub", "lane"),
        P(), P(), P(), P(), P(), P(),
    )
    return jax.shard_map(
        functools.partial(body, mesh.shape["region"], mesh.shape["sub"]),
        mesh=mesh,
        in_specs=placed,
        out_specs=P(None, "sub", "lane", ("groups", "region")),
        check_vma=False,
    )
```

time: 145 us -> 24 us (0.17)
  local copies, waits for them, and re-layouts: 49.7 us -> 5.14 us
  waiting for transfers between devices: 43.2 us -> 0 us
  starting transfers between devices: 24.1 us -> 0 us
  matrix products: 19.7 us -> 0 us
  Pallas kernels: 0 us -> 17.9 us
  other arithmetic: 6.34 us -> 0 us
    ppermute x12 -> x0, waiting for transfers between devices: 43.2 us -> none  [the longest x6 22.2 us: extended(): before = lax.ppermute(last, axis, up)]
    conv_general_dilated x10 -> x0, local copies, waits for them, and re-layouts: 40.7 us -> none  [dense_layer(): lax.conv_general_dilated(padded[None], kernel, (1, 1, 1), 'VALID', prefer...]
    ppermute x12 -> x0, starting transfers between devices: 24.1 us -> none  [the longest x6 16.2 us: extended(): before = lax.ppermute(last, axis, up)]
    conv_general_dilated x2 -> x0, matrix products: 19.7 us -> none  [dense_layer(): lax.conv_general_dilated(padded[None], kernel, (1, 1, 1), 'VALID', prefer...]
    pallas_call x0 -> x1, Pallas kernels: none -> 17.9 us  [body(): pl.pallas_call(functools.partial(kernel, n_region, n_sub), out_shape=jax....]
    convert_element_type x3 -> x0, other arithmetic: 2.19 us -> none  [the longest x1 1.18 us: body(): return summed.astype(jnp.bfloat16)]
    unnamed x20 -> x19, local copies, waits for them, and re-layouts: 6.52 us -> 5.14 us
  transfers between devices with their start and end apart: 12 -> 0, of which waited for: 10 -> 0; matrix products, arithmetic and copies ran while one was open for 0% -> 0% of each run, Pallas kernels for 0% -> 0%
where the time goes in v1:
time: 24 us; the launch traced here: 23.7 us
  Pallas kernels  17.9 us (75%)
  local copies, waits for them, and re-layouts  5.14 us (21%)
  between operations  0.71 us (3%)
    pallas_call x1, Pallas kernels, body(): pl.pallas_call(functools.partial(kernel, n_region, n_sub), out_shape=jax....  17.9 us
    unnamed x19, local copies, waits for them, and re-layouts  5.14 us

profile of v1, /device:TPU:0, one launch (start us, length us, event | category | flops | bytes accessed | tf_op | source)
XLA Modules:
  0.0 23.7 jit_solution(15674535557725477076)
XLA Ops:
  0.7 0.0 copy-start.7
  0.7 0.0 copy-start.8
  0.7 0.0 copy-start.4
  0.7 0.0 copy-start.5
  0.7 0.0 copy-start.6
  0.7 0.6 %copy-done.7 = f32[32]{0:T(128)S(1)} copy-done((f32[32]{0:T(128)S(1)}, f32[32]{0:T(128)}, u32[]{:S(2)}) %copy-start.7) | copy-done | bytes 152
  1.3 0.0 copy-done.8
  1.3 0.0 copy-done.4
  1.3 0.0 copy-done.5
  1.4 0.0 copy-done.6
  1.4 0.0 copy-start
  1.4 1.0 %copy-done = bf16[32,8,8,128]{3,2,1,0:T(8,128)(2,1)S(1)} copy-done((bf16[32,8,8,128]{3,2,1,0:T(8,128)(2,1)S(1)}, bf16[32,8,8,128]{3,2,1,0:T(8,128)(2,1)}, u32[]{:S(2)}) %copy-start) | copy-done | bytes 524312
  2.4 0.0 copy-start.1
  2.4 0.9 %copy-done.1 = bf16[27,32,32]{2,1,0:T(8,128)(2,1)S(1)} copy-done((bf16[27,32,32]{2,1,0:T(8,128)(2,1)S(1)}, bf16[27,32,32]{2,1,0:T(8,128)(2,1)}, u32[]{:S(2)}) %copy-start.1) | copy-done | bytes 55320
  3.4 0.0 copy-start.2
  3.4 0.9 %copy-done.2 = bf16[27,32,32]{2,1,0:T(8,128)(2,1)S(1)} copy-done((bf16[27,32,32]{2,1,0:T(8,128)(2,1)S(1)}, bf16[27,32,32]{2,1,0:T(8,128)(2,1)}, u32[]{:S(2)}) %copy-start.2) | copy-done | bytes 55320
  4.3 0.0 copy-start.3
  4.3 0.8 %copy-done.3 = s32[8,8,128]{2,1,0:T(8,128)S(1)} copy-done((s32[8,8,128]{2,1,0:T(8,128)S(1)}, s32[8,8,128]{2,1,0:T(8,128)}, u32[]{:S(2)}) %copy-start.3) | copy-done | bytes 32792
  5.0 17.9 %shard_map.100 = bf16[32,8,8,128]{3,2,1,0:T(8,128)(2,1)S(1)} custom-call(bf16[32,8,8,128]{3,2,1,0:T(8,128)(2,1)S(1)} %copy-done, s32[8,8,128]{2,1,0:T(8,128)S(1)} %copy-done.3, s32[1,1,1,8]{3,2,1,0:T(1,128)S(1)} %copy-done.4, s32[1,1,1]{2,1,0:T(1,128)S(6)} %copy.12.count, bf16[27,32,32]{2,1,0:T(8,128)(2,1)S(1)} %copy-done.1, f32[1,32]{1,0:T(1,128)S(1)} %bitcast.4, ...), custom_call_target="tpu_custom_call" | custom-call | tf_op jit(solution)/shard_map/pallas_call | solution.py:275
  22.9 0.8 %copy.13 = bf16[32,8,8,128]{3,2,1,0:T(8,128)(2,1)} copy(bf16[32,8,8,128]{3,2,1,0:T(8,128)(2,1)S(1)} %shard_map.100) | data formatting | bytes 1048576
Async XLA Ops:
  0.7 0.7 %copy-start.7 = (f32[32]{0:T(128)S(1)}, f32[32]{0:T(128)}, u32[]{:S(2)}) copy-start(f32[32]{0:T(128)} %param.18) | copy-start | bytes 388
  0.7 0.7 %copy-start.8 = (f32[32]{0:T(128)S(1)}, f32[32]{0:T(128)}, u32[]{:S(2)}) copy-start(f32[32]{0:T(128)} %param.19) | copy-start | bytes 388
  0.7 0.7 %copy-start.4 = (s32[1,1,1,8]{3,2,1,0:T(1,128)S(1)}, s32[1,1,1,8]{3,2,1,0:T(1,128)}, u32[]{:S(2)}) copy-start(s32[1,1,1,8]{3,2,1,0:T(1,128)} %bricks.1) | copy-start | bytes 100
  0.7 0.7 %copy-start.5 = (f32[32]{0:T(128)S(1)}, f32[32]{0:T(128)}, u32[]{:S(2)}) copy-start(f32[32]{0:T(128)} %param.15) | copy-start | bytes 388
  0.7 0.7 %copy-start.6 = (f32[32]{0:T(128)S(1)}, f32[32]{0:T(128)}, u32[]{:S(2)}) copy-start(f32[32]{0:T(128)} %param.16) | copy-start | bytes 388
  1.4 1.0 %copy-start = (bf16[32,8,8,128]{3,2,1,0:T(8,128)(2,1)S(1)}, bf16[32,8,8,128]{3,2,1,0:T(8,128)(2,1)}, u32[]{:S(2)}) copy-start(bf16[32,8,8,128]{3,2,1,0:T(8,128)(2,1)} %feat.1) | copy-start | bytes 1572868
  2.4 0.9 %copy-start.1 = (bf16[27,32,32]{2,1,0:T(8,128)(2,1)S(1)}, bf16[27,32,32]{2,1,0:T(8,128)(2,1)}, u32[]{:S(2)}) copy-start(bf16[27,32,32]{2,1,0:T(8,128)(2,1)} %w1.1) | copy-start | bytes 165892
  3.4 0.9 %copy-start.2 = (bf16[27,32,32]{2,1,0:T(8,128)(2,1)S(1)}, bf16[27,32,32]{2,1,0:T(8,128)(2,1)}, u32[]{:S(2)}) copy-start(bf16[27,32,32]{2,1,0:T(8,128)(2,1)} %w2.1) | copy-start | bytes 165892
  4.3 0.8 %copy-start.3 = (s32[8,8,128]{2,1,0:T(8,128)S(1)}, s32[8,8,128]{2,1,0:T(8,128)}, u32[]{:S(2)}) copy-start(s32[8,8,128]{2,1,0:T(8,128)} %occ.1) | copy-start | bytes 98308

commit v2 on v1

--- a/solution.py
+++ b/solution.py
@@ -34,8 +34,8 @@
 
 def kernel(
     n_region, n_sub,
-    feat, occ, bricks, count, w1, s1, h1, w2, s2, h2, out,
-    D, DY, B, BY, BC, WC, ACC, G, ACT, SX, SY, SZ, RX, RY, RZ, send_sem, recv_sem,
+    feat_hbm, occ_hbm, bricks_hbm, count_hbm, w1_hbm, s1_hbm, h1_hbm, w2_hbm, s2_hbm, h2_hbm, out,
+    feat, occ, bricks, count, w1, s1, h1, w2, s2, h2, load_sem, DX, D, DY, B, BY, BC, WC, ACC, G, ACT, SX, SY, SZ, RX, RY, RZ, send_sem, recv_sem,
 ):
     r = lax.axis_index("region")
     s = lax.axis_index("sub")
@@ -50,8 +50,18 @@
     def target(dr, ds, dl):
         return {"region": r + dr, "sub": s + ds, "lane": 1 - l if dl else l}
 
+    pairs = [
+        (count_hbm, count), (bricks_hbm, bricks), (occ_hbm, occ), (feat_hbm, feat), (w1_hbm, w1), (w2_hbm, w2),
+        (s1_hbm, s1), (h1_hbm, h1), (s2_hbm, s2), (h2_hbm, h2),
+    ]
+    loads = [pltpu.make_async_copy(a, b, load_sem.at[i]) for i, (a, b) in enumerate(pairs)]
+    for load in loads:
+        load.start()
     barrier = pltpu.get_barrier_semaphore()
     RX[...] = jnp.zeros_like(RX)
+    for rnd in range(2):
+        D[rnd, 0, :, :, pl.ds(0, 128)] = jnp.zeros((3, 256, 128), BF)
+        D[rnd, 5, :, :, pl.ds(128, 128)] = jnp.zeros((3, 256, 128), BF)
     RY[...] = jnp.zeros_like(RY)
     RZ[...] = jnp.zeros_like(RZ)
     for kind in KINDS:
@@ -78,17 +88,23 @@
             device_id=target(dr, ds, dl), device_id_type=MESH,
         )
 
-    def send(rnd):
+    def group(kind):
+        dr, ds, dl = kind
+        return "z" if dr else "x" if not dl else "edge" if ds else "y"
+
+    def send(rnd, which):
         for k, (dr, ds, dl) in enumerate(KINDS):
-            @pl.when(inside(dr, ds))
-            def _(k=k):
-                message(rnd, k).start()
-
-    def arrived(rnd):
+            if group(KINDS[k]) in which:
+                @pl.when(inside(dr, ds))
+                def _(k=k):
+                    message(rnd, k).start()
+
+    def arrived(rnd, which):
         for k, (dr, ds, dl) in enumerate(KINDS):
-            @pl.when(inside(-dr, -ds))
-            def _(k=k):
-                message(rnd, k).wait_recv()
+            if group(KINDS[k]) in which:
+                @pl.when(inside(-dr, -ds))
+                def _(k=k):
+                    message(rnd, k).wait_recv()
 
     def sent(rnd):
         for k, (dr, ds, dl) in enumerate(KINDS):
@@ -96,6 +112,8 @@
             def _(k=k):
                 message(rnd, k).wait_send()
 
+    for load in loads[:4]:
+        load.wait()
     lane128 = iota((8, 128), 1)
     slot = lane128 >> 3
     live = jnp.zeros((8, 128), F32)
@@ -148,15 +166,17 @@
             SY[rnd, pl.ds(x * 32, 32)] = dot(pick_edge, v).astype(BF)
         SZ[rnd] = columns.astype(BF)
 
-    for x in range(8):
+    def span(at, size):
+        return 1 + jnp.where(at > 0, 1, 0) + jnp.where(at < size - 1, 1, 0)
+
+    for x in (0, 7, 1, 2, 3, 4, 5, 6):
         v = feat[:, x].astype(F32) * ACT[x][None]
         put_plane(0, x, v.reshape(256, 128))
     pack(0)
-    def span(at, size):
-        return 1 + jnp.where(at > 0, 1, 0) + jnp.where(at < size - 1, 1, 0)
-
     pl.semaphore_wait(barrier, span(r, n_region) * span(s, n_sub) * 2 - 1)
-    send(0)
+    send(0, ("z",))
+    send(0, ("x",))
+    send(0, ("edge", "y"))
 
     ri = iota((256, 256), 0)
     rj = iota((256, 256), 1)
@@ -194,8 +214,9 @@
                 side += dot(tap, onehot(pj == pi + 32 * (dx * 3 + dz)))
         BY[layer] = dot(put_edge, side.astype(BF)).astype(BF)
 
+    for load in loads[4:]:
+        load.wait()
     build(0, w1)
-    build(1, w2)
 
     si = iota((96, 96), 0)
     sj = iota((96, 96), 1)
@@ -214,17 +235,35 @@
     def main(layer, xx):
         return dot(B[layer], D[layer, pl.ds(xx, 3)].reshape(2304, 256))
 
+    def put_rows(layer, x):
+        three = shifted(RY[layer, pl.ds((x + 1) * 32, 32)].astype(F32))
+        for p, h in places(x):
+            for dz in range(3):
+                DY[layer, pl.ds(p * 96 + dz * 32, 32), pl.ds(h * 128, 128)] = three[dz]
+
+    def add_rows(layer, xx):
+        ACC[xx] += dot(BY[layer], DY[layer, pl.ds(xx * 96, 288)])
+
     def layer_sums(layer):
-        for xx in (1, 2):
-            ACC[xx] = main(layer, xx)
-        arrived(layer)
-        for x, side in ((-1, 0), (8, 1)):
-            put_plane(layer, x, RX[layer, side].astype(F32))
-        for x in range(-1, 9):
-            three = shifted(RY[layer, pl.ds((x + 1) * 32, 32)].astype(F32))
-            for p, h in places(x):
-                for dz in range(3):
-                    DY[layer, pl.ds(p * 96 + dz * 32, 32), pl.ds(h * 128, 128)] = three[dz]
+        arrived(layer, ("y",))
+        for x in range(8):
+            put_rows(layer, x)
+        add_rows(layer, 1)
+        add_rows(layer, 2)
+        arrived(layer, ("x",))
+        for side, xx, first_row in ((0, 0, 0), (1, 3, 1536)):
+            three = shifted(RX[layer, side].astype(F32))
+            for dz in range(3):
+                DX[side, dz] = three[dz]
+            ACC[xx, :, pl.ds(side * 128, 128)] += dot(
+                B[layer, :, pl.ds(first_row, 768)], DX[side].reshape(768, 128)
+            )
+        arrived(layer, ("edge",))
+        put_rows(layer, -1)
+        put_rows(layer, 8)
+        add_rows(layer, 0)
+        add_rows(layer, 3)
+        arrived(layer, ("z",))
         own = dot(place, RZ[layer, 0]).astype(BF)
         other = dot(place, RZ[layer, 1]).astype(BF)
         total = jnp.zeros((256, 16), F32)
@@ -237,8 +276,7 @@
     ends = (zl == 0) | (zl == 127)
 
     def finish(layer, xx, scale, shift):
-        acc = ACC[xx] if xx in (1, 2) else main(layer, xx)
-        acc = acc + dot(BY[layer], DY[layer, pl.ds(xx * 96, 288)])
+        acc = ACC[xx]
         got = []
         for h in range(2):
             x = xx + 4 * h
@@ -248,14 +286,22 @@
             got.append((x, v))
         return got
 
+    for xx in range(4):
+        ACC[xx] = main(0, xx)
+    build(1, w2)
     layer_sums(0)
     scale, shift = rows_of(s1), rows_of(h1)
     for xx in (0, 3, 1, 2):
         for x, v in finish(0, xx, scale, shift):
             put_plane(1, x, v.reshape(256, 128).astype(BF).astype(F32))
+        if xx == 3:
+            send(1, ("x",))
     pack(1)
-    send(1)
-
+    send(1, ("z",))
+    send(1, ("edge", "y"))
+
+    for xx in range(4):
+        ACC[xx] = main(1, xx)
     layer_sums(1)
     scale, shift = rows_of(s2), rows_of(h2)
     for xx in (1, 2, 0, 3):
@@ -271,13 +317,26 @@
 def body(n_region, n_sub, features, occupancy, brick_list, brick_count, w1, s1, h1, w2, s2, h2):
     assert features.shape == (32, 8, 8, 128)
     vmem = pl.BlockSpec(memory_space=pltpu.VMEM)
-    smem = pl.BlockSpec(memory_space=pltpu.SMEM)
+    hbm = pl.BlockSpec(memory_space=pltpu.HBM)
+    scales = [v.reshape(1, -1) for v in (s1, h1, s2, h2)]
     return pl.pallas_call(
         functools.partial(kernel, n_region, n_sub),
         out_shape=jax.ShapeDtypeStruct(features.shape, BF),
-        in_specs=[vmem, vmem, smem, smem] + [vmem] * 6,
+        in_specs=[hbm] * 10,
         out_specs=vmem,
         scratch_shapes=[
+            pltpu.VMEM(features.shape, BF),
+            pltpu.VMEM(occupancy.shape, jnp.int32),
+            pltpu.SMEM(brick_list.shape, jnp.int32),
+            pltpu.SMEM(brick_count.shape, jnp.int32),
+            pltpu.VMEM(w1.shape, BF),
+            pltpu.VMEM((1, 32), F32),
+            pltpu.VMEM((1, 32), F32),
+            pltpu.VMEM(w2.shape, BF),
+            pltpu.VMEM((1, 32), F32),
+            pltpu.VMEM((1, 32), F32),
+            pltpu.SemaphoreType.DMA((10,)),
+            pltpu.VMEM((2, 3, 256, 128), BF),
             pltpu.VMEM((2, 6, 3, 256, 256), BF),
             pltpu.VMEM((2, 576, 256), BF),
             pltpu.VMEM((2, 256, 2304), BF),
@@ -297,9 +356,9 @@
             pltpu.SemaphoreType.DMA((2, len(KINDS))),
         ],
         compiler_params=pltpu.CompilerParams(
-            collective_id=0, has_side_effects=True, vmem_limit_bytes=48 * 1024 * 1024
+            collective_id=0, has_side_effects=True, vmem_limit_bytes=64000 * 1024
         ),
-    )(features, occupancy, brick_list, brick_count, w1, s1.reshape(1, -1), h1.reshape(1, -1), w2, s2.reshape(1, -1), h2.reshape(1, -1))
+    )(features, occupancy, brick_list, brick_count, w1, scales[0], scales[1], w2, scales[2], scales[3])
 
 
 def solution(mesh):

time: 24 us -> 20.9 us (0.87)
  local copies, waits for them, and re-layouts: 5.14 us -> 1.87 us
  Pallas kernels: 17.9 us -> 18.2 us
    unnamed x19 -> x1, local copies, waits for them, and re-layouts: 5.14 us -> 1.87 us
    pallas_call x1, Pallas kernels: 17.9 us -> 18.2 us  [body(): pl.pallas_call(functools.partial(kernel, n_region, n_sub), out_shape=jax....]
where the time goes in v2:
time: 20.9 us; the launch traced here: 20.8 us
  Pallas kernels  18.2 us (87%)
  local copies, waits for them, and re-layouts  1.87 us (9%)
  between operations  0.66 us (3%)
    pallas_call x1, Pallas kernels, body(): pl.pallas_call(functools.partial(kernel, n_region, n_sub), out_shape=jax....  18.2 us
    unnamed x1, local copies, waits for them, and re-layouts  1.87 us

profile of v2, /device:TPU:0, one launch (start us, length us, event | category | flops | bytes accessed | tf_op | source)
XLA Modules:
  0.0 20.8 jit_solution(6477396577622819035)
XLA Ops:
  0.7 18.2 %shard_map.100 = bf16[32,8,8,128]{3,2,1,0:T(8,128)(2,1)} custom-call(bf16[32,8,8,128]{3,2,1,0:T(8,128)(2,1)} %feat_hbm.1, s32[8,8,128]{2,1,0:T(8,128)} %occ_hbm.1, s32[1,1,1,8]{3,2,1,0:T(1,128)} %bricks_hbm.1, s32[1,1,1]{2,1,0:T(1,128)S(6)} %copy.12.count_hbm, bf16[27,32,32]{2,1,0:T(8,128)(2,1)} %w1_hbm.1, f32[1,32]{1,0:T(1,128)} %bitcast.4, ...), custom_call_target="tpu_custom_call" | custom-call | tf_op jit(solution)/shard_map/pallas_call | solution.py:322
  18.9 1.9 %copy.13 = bf16[32,8,8,128]{3,2,1,0:T(8,128)(2,1)} copy(bf16[32,8,8,128]{3,2,1,0:T(8,128)(2,1)} %shard_map.100) | data formatting | bytes 1048576

commit v3 on v2

--- a/solution.py
+++ b/solution.py
@@ -34,8 +34,8 @@
 
 def kernel(
     n_region, n_sub,
-    feat_hbm, occ_hbm, bricks_hbm, count_hbm, w1_hbm, s1_hbm, h1_hbm, w2_hbm, s2_hbm, h2_hbm, out,
-    feat, occ, bricks, count, w1, s1, h1, w2, s2, h2, load_sem, DX, D, DY, B, BY, BC, WC, ACC, G, ACT, SX, SY, SZ, RX, RY, RZ, send_sem, recv_sem,
+    feat_hbm, occ_hbm, bricks_hbm, count_hbm, w1_hbm, s1_hbm, h1_hbm, w2_hbm, s2_hbm, h2_hbm, out_hbm,
+    feat, occ, bricks, count, w1, s1, h1, w2, s2, h2, load_sem, out, out_sem, DX, D, DY, B, BY, BC, WC, ACC, G, ACT, SX, SY, SZ, RX, RY, RZ, send_sem, recv_sem,
 ):
     r = lax.axis_index("region")
     s = lax.axis_index("sub")
@@ -173,11 +173,6 @@
         v = feat[:, x].astype(F32) * ACT[x][None]
         put_plane(0, x, v.reshape(256, 128))
     pack(0)
-    pl.semaphore_wait(barrier, span(r, n_region) * span(s, n_sub) * 2 - 1)
-    send(0, ("z",))
-    send(0, ("x",))
-    send(0, ("edge", "y"))
-
     ri = iota((256, 256), 0)
     rj = iota((256, 256), 1)
     order = onehot((ri >> 3 == (rj & 31)) & ((ri & 7) == (rj >> 5)))
@@ -218,6 +213,12 @@
         load.wait()
     build(0, w1)
 
+    pl.semaphore_wait(barrier, span(r, n_region) * span(s, n_sub) * 2 - 1)
+    send(0, ("z",))
+    send(0, ("x",))
+    send(0, ("edge", "y"))
+
+
     si = iota((96, 96), 0)
     sj = iota((96, 96), 1)
     q, j = si >> 4, si & 15
@@ -310,20 +311,22 @@
             begin = D[0, p, 1, :, pl.ds(h * 128, 128)].astype(F32).reshape(32, 8, 128)
             v = (v.astype(BF).astype(F32) + begin) * ACT[x][None]
             out[:, x] = v.astype(BF)
+            pltpu.make_async_copy(out.at[:, x], out_hbm.at[:, x], out_sem.at[x]).start()
     sent(0)
     sent(1)
+    for x in range(8):
+        pltpu.make_async_copy(out.at[:, x], out_hbm.at[:, x], out_sem.at[x]).wait()
 
 
 def body(n_region, n_sub, features, occupancy, brick_list, brick_count, w1, s1, h1, w2, s2, h2):
     assert features.shape == (32, 8, 8, 128)
-    vmem = pl.BlockSpec(memory_space=pltpu.VMEM)
     hbm = pl.BlockSpec(memory_space=pltpu.HBM)
     scales = [v.reshape(1, -1) for v in (s1, h1, s2, h2)]
     return pl.pallas_call(
         functools.partial(kernel, n_region, n_sub),
         out_shape=jax.ShapeDtypeStruct(features.shape, BF),
         in_specs=[hbm] * 10,
-        out_specs=vmem,
+        out_specs=hbm,
         scratch_shapes=[
             pltpu.VMEM(features.shape, BF),
             pltpu.VMEM(occupancy.shape, jnp.int32),
@@ -336,6 +339,8 @@
             pltpu.VMEM((1, 32), F32),
             pltpu.VMEM((1, 32), F32),
             pltpu.SemaphoreType.DMA((10,)),
+            pltpu.VMEM(features.shape, BF),
+            pltpu.SemaphoreType.DMA((8,)),
             pltpu.VMEM((2, 3, 256, 128), BF),
             pltpu.VMEM((2, 6, 3, 256, 256), BF),
             pltpu.VMEM((2, 576, 256), BF),

time: 20.9 us -> 20.8 us (level)
  no operation moved by 1% of the time
where the time goes in v3:
time: 20.8 us; the launch traced here: 20.6 us
  Pallas kernels  18.1 us (87%)
  local copies, waits for them, and re-layouts  1.87 us (9%)
  between operations  0.66 us (3%)
    pallas_call x1, Pallas kernels, body(): pl.pallas_call(functools.partial(kernel, n_region, n_sub), out_shape=jax....  18.1 us
    unnamed x1, local copies, waits for them, and re-layouts  1.87 us

profile of v3, /device:TPU:0, one launch (start us, length us, event | category | flops | bytes accessed | tf_op | source)
XLA Modules:
  0.0 20.6 jit_solution(15525952177607739427)
XLA Ops:
  0.7 18.1 %shard_map.100 = bf16[32,8,8,128]{3,2,1,0:T(8,128)(2,1)} custom-call(bf16[32,8,8,128]{3,2,1,0:T(8,128)(2,1)} %feat_hbm.1, s32[8,8,128]{2,1,0:T(8,128)} %occ_hbm.1, s32[1,1,1,8]{3,2,1,0:T(1,128)} %bricks_hbm.1, s32[1,1,1]{2,1,0:T(1,128)S(6)} %copy.12.count_hbm, bf16[27,32,32]{2,1,0:T(8,128)(2,1)} %w1_hbm.1, f32[1,32]{1,0:T(1,128)} %bitcast.4, ...), custom_call_target="tpu_custom_call" | custom-call | tf_op jit(solution)/shard_map/pallas_call | solution.py:325
  18.7 1.9 %copy.13 = bf16[32,8,8,128]{3,2,1,0:T(8,128)(2,1)} copy(bf16[32,8,8,128]{3,2,1,0:T(8,128)(2,1)} %shard_map.100) | data formatting | bytes 1048576
